TPU v7x, 32 devices: a whole 2x2x4 slice. The times are simulated.
32 devices in a mesh: group: 2 (over y), out: 4 (over z), inp: 2 (over x), dp: 2 (over core).
Axes of the slice: x: 2, y: 2, z: 4, core: 2. Of those that a mesh axis runs over, the one named last changes fastest.
Arguments:
- activations: bfloat16 [16, 128, 8192], P(('group', 'dp'), 'out', 'inp'), parts along dimension 0, may hold values from -6 to 6
- out_grads: bfloat16 [16, 128, 28672], P(('group', 'dp'), 'inp', 'out'), parts along dimension 0, may hold values from -6 to 6
- basis_in: bfloat16 [8192, 4096], P('inp', 'out'), may hold values from -0.0625 to 0.0625
- basis_out: bfloat16 [28672, 14336], P('out', ('inp', 'dp')), may hold values from -0.03125 to 0.03125
Outputs:
- eigenvalues: float32 [8192, 14336], P(('group', 'out'), ('inp', 'dp')), parts along dimension 0
There are 2 independent parts, one for each index of `group`. A program takes and returns all parts, laid end to end along the dimension named above; an argument that names none is the same for every part. Nothing has to cross between parts.
All inputs are finite; a program needn't handle non-finite values.
Results may differ from a plain program's by a relative error of at most 0.0028.
Values may be sent and summed in bfloat16 or wider, within the bound.
A program may use at most 256 MiB of HBM per device.

v0:
```python
import jax
import jax.numpy as jnp
from jax import lax
from jax.sharding import PartitionSpec as P


def body(activations, out_grads, basis_in, basis_out):
    gathered_grads = lax.all_gather(out_grads, "dp", axis=0, tiled=True)
    grad_partial = jnp.einsum(
        "etf,fk->etk",
        lax.all_gather(gathered_grads, "inp", axis=1, tiled=True),
        basis_out,
        preferred_element_type=jnp.float32,
    )
    grad_hat = lax.psum(grad_partial, "out").astype(jnp.bfloat16)
    gathered_acts = lax.all_gather(activations, "dp", axis=0, tiled=True)
    act_partial = jnp.einsum(
        "etd,dk->etk",
        lax.all_gather(gathered_acts, "out", axis=1, tiled=True),
        basis_in,
        preferred_element_type=jnp.float32,
    )
    act_hat = lax.psum(act_partial, "inp").astype(jnp.bfloat16)
    rotated = jnp.einsum("etd,etf->edf", act_hat, grad_hat, preferred_element_type=jnp.float32)
    count_rows = act_hat.shape[0] * act_hat.shape[1]
    return jnp.sum(rotated * rotated, axis=0) / count_rows


def solution(mesh):
    placed = (
        P(("group", "dp"), "out", "inp"),
        P(("group", "dp"), "inp", "out"),
        P("inp", "out"),
        P("out", ("inp", "dp")),
    )
    return jax.shard_map(
        body,
        mesh=mesh,
        in_specs=placed,
        out_specs=P(("group", "out"), ("inp", "dp")),
        check_vma=False,
    )
```

profile of v0, /device:TPU:0, one launch (start us, length us, event | category | flops | bytes accessed | tf_op | source)
XLA Modules:
  0.0 1059.9 jit_solution(17323243078708015453)
XLA Ops:
  6.5 0.0 all-gather.5.cloned.1.call-start
  6.5 0.7 all-gather.5.cloned.1.call-update
  7.3 0.0 all-gather.9.cloned.1.call-start
  7.3 0.7 all-gather.9.cloned.1.call-update
  8.0 0.0 all-gather.7.cloned.1.call-start
  8.1 14.2 %all-gather.5.cloned.1.call-done = bf16[8,32,4096]{2,1,0:T(8,128)(2,1)} async-done(((bf16[4,32,4096]{2,1,0:T(8,128)(2,1)}), bf16[8,32,4096]{2,1,0:T(8,128)(2,1)}) %all-gather.5.cloned.1.call-update) | async-done | bytes 2097168 | tf_op jit(solution)/shard_map/all_gather | solution.py:16
  22.2 0.0 all-gather.7.cloned.1.call-update
  22.2 0.0 all-gather.11.cloned.1.call-start
  22.3 21.0 %all-gather.9.cloned.1.call-done = bf16[8,64,7168]{2,1,0:T(8,128)(2,1)} async-done(((bf16[4,64,7168]{2,1,0:T(8,128)(2,1)}), bf16[8,64,7168]{2,1,0:T(8,128)(2,1)}) %all-gather.9.cloned.1.call-update) | async-done | bytes 7340048 | tf_op jit(solution)/shard_map/all_gather | solution.py:8
  43.3 0.0 all-gather.11.cloned.1.call-update
  43.3 152.4 %all-gather.7.cloned.1.call-done = bf16[8,128,4096]{2,1,0:T(8,128)(2,1)} async-done(((bf16[8,32,4096]{2,1,0:T(8,128)(2,1)}), bf16[8,128,4096]{2,1,0:T(8,128)(2,1)}) %all-gather.7.cloned.1.call-update) | async-done | bytes 8388624 | tf_op jit(solution)/shard_map/all_gather | solution.py:19
  195.7 15.0 %fusion.2 = f32[8,128,1024]{1,2,0:T(8,128)} fusion(bf16[8,128,4096]{2,1,0:T(8,128)(2,1)} %all-gather.7.cloned.1.call-done, bf16[4096,1024]{1,0:T(8,128)(2,1)} %param.6), kind=kOutput, calls=%fused_computation.3 | convolution fusion | flops 8589934592 | bytes 20971520 | tf_op jit(solution)/shard_map/etd,dk->etk/dot_general | solution.py:17
  210.7 192.7 %all-reduce.2 = bf16[8,128,1024]{1,2,0:T(8,128)(2,1)S(1)} all-reduce(f32[8,128,1024]{1,2,0:T(8,128)} %fusion.2), channel_id=1, replica_groups=mesh['group'=2,'out'=4,'inp'=2,'dp'=2] {'inp'}, use_global_device_ids=true, to_apply=%region_0.0 | all-reduce | flops 1048576 | bytes 6291456 | tf_op jit(solution)/shard_map/psum | solution.py:23
  403.4 57.0 %all-gather.11.cloned.1.call-done = bf16[8,128,7168]{2,1,0:T(8,128)(2,1)} async-done(((bf16[8,64,7168]{2,1,0:T(8,128)(2,1)}), bf16[8,128,7168]{2,1,0:T(8,128)(2,1)}) %all-gather.11.cloned.1.call-update) | async-done | bytes 14680080 | tf_op jit(solution)/shard_map/all_gather | solution.py:11
  460.4 62.7 %fusion = f32[8,128,3584]{2,1,0:T(8,128)} fusion(bf16[8,128,7168]{2,1,0:T(8,128)(2,1)} %all-gather.11.cloned.1.call-done, bf16[7168,3584]{1,0:T(8,128)(2,1)} %param.7), kind=kOutput, calls=%fused_computation.1 | convolution fusion | flops 52613349376 | bytes 80740352 | tf_op jit(solution)/shard_map/etf,fk->etk/dot_general | solution.py:9
  523.1 492.7 %all-reduce.3 = bf16[8,128,3584]{2,1,0:T(8,128)(2,1)} all-reduce(f32[8,128,3584]{2,1,0:T(8,128)} %fusion), channel_id=1, replica_groups=mesh['group'=2,'out'=4,'inp'=2,'dp'=2] {'out'}, use_global_device_ids=true, to_apply=%region_1.0 | all-reduce | flops 3670016 | bytes 22020096 | tf_op jit(solution)/shard_map/psum | solution.py:15
  1015.7 25.5 %multiply_reduce_fusion = f32[1024,3584]{1,0:T(8,128)} fusion(bf16[8,128,3584]{2,1,0:T(8,128)(2,1)} %all-reduce.3, bf16[8,128,1024]{1,2,0:T(8,128)(2,1)S(1)} %all-reduce.2), kind=kOutput, calls=%fused_computation | convolution fusion | flops 7571243008 | bytes 24117248 | tf_op jit(solution)/shard_map/etd,etf->edf/dot_general | solution.py:24
  1041.2 12.2 %broadcast_multiply_fusion = f32[1024,3584]{1,0:T(8,128)} fusion(f32[1024,3584]{1,0:T(8,128)} %multiply_reduce_fusion), kind=kLoop, calls=%fused_computation.5 | loop fusion | flops 3670016 | bytes 29360128 | tf_op jit(solution)/shard_map/div | solution.py:26
Async XLA Ops:
  6.5 15.7 %all-gather.5.cloned.1.call-start = ((), (), s32[]{:S(2)}) async-start(), calls=%async_computation | async-start | bytes 3145728 | tf_op jit(solution)/shard_map/all_gather | solution.py:16
  7.3 36.0 %all-gather.9.cloned.1.call-start = ((), (), s32[]{:S(2)}) async-start(), calls=%async_computation.2 | async-start | bytes 11010048 | tf_op jit(solution)/shard_map/all_gather | solution.py:8
  8.0 187.7 %all-gather.7.cloned.1.call-start = ((), (), s32[]{:S(2)}) async-start(), calls=%async_computation.1 | async-start | bytes 10485760 | tf_op jit(solution)/shard_map/all_gather | solution.py:19
  22.2 438.1 %all-gather.11.cloned.1.call-start = ((), (), s32[]{:S(2)}) async-start(), calls=%async_computation.3 | async-start | bytes 22020096 | tf_op jit(solution)/shard_map/all_gather | solution.py:11
Sparse Core Ops, SparseCore 0:
  8.9 13.2 all-gather.4
  23.7 19.4 all-gather.8
  44.8 150.7 all-gather.6
  197.1 263.2 all-gather.10
where the time goes:
time: 1060 us
  blocking collectives  685 us (65%)
  waiting for transfers between devices  246 us (23%)
  matrix products  103 us (10%)
  between operations  13.1 us (1%)
  other arithmetic  12.2 us (1%)
    psum x1, blocking collectives, body(): grad_hat = lax.psum(grad_partial, 'out').astype(jnp.bfloat16)  493 us
    psum x1, blocking collectives, body(): act_hat = lax.psum(act_partial, 'inp').astype(jnp.bfloat16)  193 us
    all_gather x1, waiting for transfers between devices, body(): lax.all_gather(gathered_acts, 'out', axis=1, tiled=True)  152 us
    dot_general x1, matrix products, body(): jnp.einsum('etf,fk->etk', lax.all_gather(gathered_grads, 'inp', axis=1, t...  62.7 us
    all_gather x1, waiting for transfers between devices, body(): lax.all_gather(gathered_grads, 'inp', axis=1, tiled=True)  57 us
    dot_general x1, matrix products, body(): jnp.einsum('etd,etf->edf', act_hat, grad_hat, preferred_element_type=jnp....  25.5 us
  transfers between devices with their start and end apart: 4, of which 4 were waited for; matrix products, arithmetic and copies ran while one was open for 1% of the time, Pallas kernels for 0%

commit v1 on v0

v1 whole, which is shorter than its diff:
```python
import jax
import jax.numpy as jnp
from jax import lax
from jax.sharding import PartitionSpec as P

BF16 = jnp.bfloat16
F32 = jnp.float32


def sum_on_line(partial, axis, n):
    if n == 1:
        return partial.astype(BF16)
    if n % 2:
        return lax.psum(partial, axis).astype(BF16)
    me = lax.axis_index(axis)
    half = n // 2
    total = partial
    for step in range(half - 1):
        hops = [(step, step + 1), (n - 1 - step, n - 2 - step)]
        total = total + lax.ppermute(total.astype(BF16), axis, hops).astype(F32)
    swap = [(half - 1, half), (half, half - 1)]
    total = total + lax.ppermute(total.astype(BF16), axis, swap).astype(F32)
    out = total.astype(BF16)
    for step in range(half - 1):
        hops = [(half - 1 - step, half - 2 - step), (half + step, half + step + 1)]
        got = lax.ppermute(out, axis, hops)
        mine = (me == half - 2 - step) | (me == half + step + 1)
        out = jnp.where(mine, got, out)
    return out


def gather_on_line(block, axis, n):
    up = [(i, i + 1) for i in range(n - 1)]
    down = [(i + 1, i) for i in range(n - 1)]
    rights, lefts = [block], [block]
    for _ in range(n - 1):
        rights.append(lax.ppermute(rights[-1], axis, up))
        lefts.append(lax.ppermute(lefts[-1], axis, down))
    me = lax.axis_index(axis)
    slots = [block]
    for k in range(1, n):
        slots.append(jnp.where(me >= k, rights[k], lefts[n - k]))
    return slots


def make_body(n_out, n_inp, n_dp):
    def swap_dp(x):
        return lax.ppermute(x, "dp", [(0, 1), (1, 0)])

    def by_dp(mine, other):
        first = lax.axis_index("dp") == 0
        return jnp.concatenate([jnp.where(first, mine, other), jnp.where(first, other, mine)], axis=0)

    def in_order(slots, axis, n):
        me = lax.axis_index(axis)
        if n == 2:
            first = me == 0
            return [jnp.where(first, slots[0], slots[1]), jnp.where(first, slots[1], slots[0])]
        stacked = jnp.stack(slots)
        return [lax.dynamic_index_in_dim(stacked, lax.rem(me - j + n, n), 0, keepdims=False) for j in range(n)]

    def body(activations, out_grads, basis_in, basis_out):
        ex, tok, width = activations.shape
        grads = [out_grads]
        for k in range(1, n_inp):
            grads.append(lax.ppermute(out_grads, "inp", [(i, (i + k) % n_inp) for i in range(n_inp)]))
        acts = jnp.stack(gather_on_line(activations, "out", n_out))

        def project(block):
            e, t, f = block.shape
            partial = jnp.dot(block.reshape(e * t, f), basis_out, preferred_element_type=F32)
            cuts = 2 if e % 2 == 0 and (e // 2) * t % 16 == 0 else 1
            rows = e * t // cuts
            sums = [sum_on_line(partial[c * rows:(c + 1) * rows], "out", n_out) for c in range(cuts)]
            return jnp.concatenate(sums, axis=0).reshape(e, t, -1)

        mine, others = [], []
        for block in grads:
            mine.append(project(block))
            others.append(project(swap_dp(block)))

        act_partial = jnp.dot(acts.reshape(n_out * ex * tok, width), basis_in, preferred_element_type=F32)
        total = act_partial
        sent = act_partial.astype(BF16)
        for k in range(1, n_inp):
            total = total + lax.ppermute(sent, "inp", [(i, (i + k) % n_inp) for i in range(n_inp)]).astype(F32)
        act_own = total.astype(BF16).reshape(n_out, ex, tok, -1)
        act_own = jnp.concatenate(in_order([act_own[k] for k in range(n_out)], "out", n_out), axis=1)
        act_hat = by_dp(act_own, swap_dp(act_own))

        grad_mine = jnp.concatenate(in_order(mine, "inp", n_inp), axis=1)
        grad_others = jnp.concatenate(in_order(others, "inp", n_inp), axis=1)
        grad_hat = by_dp(grad_mine, grad_others)

        rotated = jnp.einsum("etd,etf->edf", act_hat, grad_hat, preferred_element_type=F32)
        count_rows = act_hat.shape[0] * act_hat.shape[1]
        return jnp.sum(rotated * rotated, axis=0) / count_rows

    return body


def solution(mesh):
    shape = dict(mesh.shape)
    placed = (
        P(("group", "dp"), "out", "inp"),
        P(("group", "dp"), "inp", "out"),
        P("inp", "out"),
        P("out", ("inp", "dp")),
    )
    return jax.shard_map(
        make_body(shape["out"], shape["inp"], shape["dp"]),
        mesh=mesh,
        in_specs=placed,
        out_specs=P(("group", "out"), ("inp", "dp")),
        check_vma=False,
    )
```

time: 1060 us -> 537 us (0.51)
  blocking collectives: 685 us -> 0 us
  starting transfers between devices: 0.12 us -> 83 us
  other arithmetic: 12.2 us -> 42.5 us
  waiting for transfers between devices: 246 us -> 272 us
  matrix products: 103 us -> 123 us
  between operations: 13.1 us -> 1.06 us
    psum x2 -> x0, blocking collectives: 685 us -> none  [the longest x1 493 us: body(): grad_hat = lax.psum(grad_partial, 'out').astype(jnp.bfloat16)]
    ppermute x0 -> x35, waiting for transfers between devices: none -> 272 us  [the longest x8 130 us: sum_on_line(): got = lax.ppermute(out, axis, hops)]
    all_gather x4 -> x0, waiting for transfers between devices: 245 us -> none  [the longest x1 152 us: body(): lax.all_gather(gathered_acts, 'out', axis=1, tiled=True)]
    ppermute x0 -> x35, starting transfers between devices: none -> 83 us  [the longest x8 37 us: sum_on_line(): total = total + lax.ppermute(total.astype(BF16), axis, hops).astype(F32)]
    dot_general x3 -> x6, matrix products: 103 us -> 123 us  [the longest x4 90.7 us: project(): jnp.dot(block.reshape(e * t, f), basis_out, preferred_element_type=F32)]
    convert_element_type x0 -> x9, other arithmetic: none -> 15.1 us  [the longest x4 8.32 us: sum_on_line(): out = total.astype(BF16)]
  transfers between devices with their start and end apart: 4 -> 35, of which waited for: 4 -> 15; matrix products, arithmetic and copies ran while one was open for 1% -> 20% of each run, Pallas kernels for 0% -> 0%
where the time goes in v1:
time: 537 us; the launch traced here: 530 us
  waiting for transfers between devices  272 us (51%)
  matrix products  123 us (23%)
  starting transfers between devices  83 us (15%)
  other arithmetic  42.5 us (8%)
  local copies, waits for them, and re-layouts  8.88 us (2%)
    ppermute x8, waiting for transfers between devices, sum_on_line(): got = lax.ppermute(out, axis, hops)  130 us
    ppermute x8, waiting for transfers between devices, sum_on_line(): total = total + lax.ppermute(total.astype(BF16), axis, hops).astype(F32)  96.8 us
    dot_general x4, matrix products, project(): jnp.dot(block.reshape(e * t, f), basis_out, preferred_element_type=F32)  90.7 us
    ppermute x8, starting transfers between devices, sum_on_line(): total = total + lax.ppermute(total.astype(BF16), axis, hops).astype(F32)  37 us
    ppermute x3, waiting for transfers between devices, gather_on_line(): lefts.append(lax.ppermute(lefts[-1], axis, down))  29.9 us
    dot_general x1, matrix products, body(): jnp.einsum('etd,etf->edf', act_hat, grad_hat, preferred_element_type=F32)  27.8 us
    ppermute x3, starting transfers between devices, gather_on_line(): rights.append(lax.ppermute(rights[-1], axis, up))  20.3 us
    ppermute x3, waiting for transfers between devices, gather_on_line(): rights.append(lax.ppermute(rights[-1], axis, up))  15.2 us
  transfers between devices with their start and end apart: 35, of which 15 were waited for; matrix products, arithmetic and copies ran while one was open for 20% of the time, Pallas kernels for 0%

profile of v1, /device:TPU:0, one launch (start us, length us, event | category | flops | bytes accessed | tf_op | source)
XLA Modules:
  0.0 530.4 jit_solution(3001591974306908065)
XLA Ops:
  0.0 22.6 %fusion.21 = f32[256,3584]{1,0:T(8,128)S(1)} fusion(bf16[256,7168]{1,0:T(8,128)(2,1)} %bitcast.13, bf16[7168,3584]{1,0:T(8,128)(2,1)} %param.7), kind=kOutput, calls=%fused_computation.80 | convolution fusion | flops 13153337344 | bytes 58720256 | tf_op jit(solution)/shard_map/dot_general | solution.py:71
  22.8 5.0 collective-permute-start.8
  30.5 5.6 %collective-permute-start = (bf16[4,32,4096]{2,1,0:T(8,128)(2,1)}, bf16[4,32,4096]{2,1,0:T(8,128)(2,1)}, u32[]{:S(2)}, u32[]{:S(2)}) collective-permute-start(bf16[4,32,4096]{2,1,0:T(8,128)(2,1)} %param.4), channel_id=1, source_target_pairs={{0,4},{4,8},{8,12},{1,5},{5,9},{9,13},{2,6},{6,10},{10,14},{3,7},{... | collective-permute-start | bytes 3145736 | tf_op jit(solution)/shard_map/ppermute | solution.py:37
  36.1 12.4 %collective-permute-done.8 = bf16[128,3584]{1,0:T(8,128)(2,1)S(1)} collective-permute-done((bf16[128,3584]{1,0:T(8,128)(2,1)S(1)}, bf16[128,3584]{1,0:T(8,128)(2,1)S(1)}, u32[]{:S(2)}, u32[]{:S(2)}) %collective-permute-start.8) | collective-permute-done | bytes 917536 | tf_op jit(solution)/shard_map/ppermute | solution.py:20
  48.5 19.7 %collective-permute-done.11 = bf16[128,3584]{1,0:T(8,128)(2,1)S(1)} collective-permute-done((bf16[128,3584]{1,0:T(8,128)(2,1)S(1)}, bf16[128,3584]{1,0:T(8,128)(2,1)S(1)}, u32[]{:S(2)}, u32[]{:S(2)}) %collective-permute-start.11) | collective-permute-done | bytes 917536 | tf_op jit(solution)/shard_map/ppermute | solution.py:20
  74.6 15.0 %collective-permute-done = bf16[4,32,4096]{2,1,0:T(8,128)(2,1)} collective-permute-done((bf16[4,32,4096]{2,1,0:T(8,128)(2,1)}, bf16[4,32,4096]{2,1,0:T(8,128)(2,1)}, u32[]{:S(2)}, u32[]{:S(2)}) %collective-permute-start) | collective-permute-done | bytes 1048608 | tf_op jit(solution)/shard_map/ppermute | solution.py:37
  90.9 9.0 %collective-permute-start.4 = (bf16[4,32,4096]{2,1,0:T(8,128)(2,1)}, bf16[4,32,4096]{2,1,0:T(8,128)(2,1)S(1)}, u32[]{:S(2)}, u32[]{:S(2)}) collective-permute-start(bf16[4,32,4096]{2,1,0:T(8,128)(2,1)} %collective-permute-done), channel_id=1, source_target_pairs={{0,4},{4,8},{8,12},{1,5},{5,9},{9,13},{2,6},{6,10},{10,14},{3,7},{... | collective-permute-start | bytes 3145736 | tf_op jit(solution)/shard_map/ppermute | solution.py:37
  99.9 3.2 add_convert_fusion.8
  104.4 11.9 %collective-permute-done.2 = bf16[4,32,4096]{2,1,0:T(8,128)(2,1)S(1)} collective-permute-done((bf16[4,32,4096]{2,1,0:T(8,128)(2,1)S(1)}, bf16[4,32,4096]{2,1,0:T(8,128)(2,1)S(1)}, u32[]{:S(2)}, u32[]{:S(2)}) %collective-permute-start.2) | collective-permute-done | bytes 1048608 | tf_op jit(solution)/shard_map/ppermute | solution.py:38
  119.2 17.4 %collective-permute-done.10 = bf16[128,3584]{1,0:T(8,128)(2,1)S(1)} collective-permute-done((bf16[128,3584]{1,0:T(8,128)(2,1)S(1)}, bf16[128,3584]{1,0:T(8,128)(2,1)S(1)}, u32[]{:S(2)}, u32[]{:S(2)}) %collective-permute-start.10) | collective-permute-done | bytes 917536 | tf_op jit(solution)/shard_map/ppermute | solution.py:26
  136.6 5.7 %collective-permute-start.5 = (bf16[4,32,4096]{2,1,0:T(8,128)(2,1)S(1)}, bf16[4,32,4096]{2,1,0:T(8,128)(2,1)S(1)}, u32[]{:S(2)}, u32[]{:S(2)}) collective-permute-start(bf16[4,32,4096]{2,1,0:T(8,128)(2,1)S(1)} %collective-permute-done.4), channel_id=1, source_target_pairs={{0,4},{4,8},{8,12},{1,5},{5,9},{9,13},{2,6},{6,10},{10,14},{3,7},{... | collective-permute-start | bytes 3145736 | tf_op jit(solution)/shard_map/ppermute | solution.py:37
  143.3 15.9 %collective-permute-done.13 = bf16[128,3584]{1,0:T(8,128)(2,1)S(1)} collective-permute-done((bf16[128,3584]{1,0:T(8,128)(2,1)S(1)}, bf16[128,3584]{1,0:T(8,128)(2,1)S(1)}, u32[]{:S(2)}, u32[]{:S(2)}) %collective-permute-start.13) | collective-permute-done | bytes 917536 | tf_op jit(solution)/shard_map/ppermute | solution.py:26
  160.4 18.0 %collective-permute-done.3 = bf16[4,32,4096]{2,1,0:T(8,128)(2,1)S(1)} collective-permute-done((bf16[4,32,4096]{2,1,0:T(8,128)(2,1)S(1)}, bf16[4,32,4096]{2,1,0:T(8,128)(2,1)S(1)}, u32[]{:S(2)}, u32[]{:S(2)}) %collective-permute-start.3) | collective-permute-done | bytes 1048608 | tf_op jit(solution)/shard_map/ppermute | solution.py:38
  181.0 4.6 fusion.20
  187.2 22.7 %fusion.23 = f32[256,3584]{1,0:T(8,128)S(1)} fusion(bf16[256,7168]{1,0:T(8,128)(2,1)} %bitcast.17, bf16[7168,3584]{1,0:T(8,128)(2,1)} %param.7), kind=kOutput, calls=%fused_computation.82 | convolution fusion | flops 13153337344 | bytes 58720256 | tf_op jit(solution)/shard_map/dot_general | solution.py:71
  211.5 3.6 collective-permute-start.22
  217.3 22.6 %fusion.22 = f32[256,3584]{1,0:T(8,128)S(1)} fusion(bf16[256,7168]{1,0:T(8,128)(2,1)} %bitcast.14, bf16[7168,3584]{1,0:T(8,128)(2,1)} %param.7), kind=kOutput, calls=%fused_computation.81 | convolution fusion | flops 13153337344 | bytes 58720256 | tf_op jit(solution)/shard_map/dot_general | solution.py:71
  244.0 2.4 collective-permute-start.18
  251.7 2.7 pad_maximum_fusion.8
  255.0 2.3 fusion.10
  258.0 16.6 %collective-permute-done.15 = bf16[128,3584]{1,0:T(8,128)(2,1)} collective-permute-done((bf16[128,3584]{1,0:T(8,128)(2,1)}, bf16[128,3584]{1,0:T(8,128)(2,1)}, u32[]{:S(2)}, u32[]{:S(2)}) %collective-permute-start.15) | collective-permute-done | bytes 917536 | tf_op jit(solution)/shard_map/ppermute | solution.py:20
  275.3 14.4 %collective-permute-done.18 = bf16[128,3584]{1,0:T(8,128)(2,1)} collective-permute-done((bf16[128,3584]{1,0:T(8,128)(2,1)}, bf16[128,3584]{1,0:T(8,128)(2,1)}, u32[]{:S(2)}, u32[]{:S(2)}) %collective-permute-start.18) | collective-permute-done | bytes 917536 | tf_op jit(solution)/shard_map/ppermute | solution.py:20
  302.9 23.4 %collective-permute-done.24 = bf16[128,3584]{1,0:T(8,128)(2,1)S(1)} collective-permute-done((bf16[128,3584]{1,0:T(8,128)(2,1)S(1)}, bf16[128,3584]{1,0:T(8,128)(2,1)S(1)}, u32[]{:S(2)}, u32[]{:S(2)}) %collective-permute-start.24) | collective-permute-done | bytes 917536 | tf_op jit(solution)/shard_map/ppermute | solution.py:26
  326.4 22.7 %fusion.24 = f32[256,3584]{1,0:T(8,128)S(1)} fusion(bf16[256,7168]{1,0:T(8,128)(2,1)} %bitcast.18, bf16[7168,3584]{1,0:T(8,128)(2,1)} %param.7), kind=kOutput, calls=%fused_computation.83 | convolution fusion | flops 13153337344 | bytes 58720256 | tf_op jit(solution)/shard_map/dot_general | solution.py:71
  349.3 18.8 %collective-permute-start.29 = (bf16[128,3584]{1,0:T(8,128)(2,1)S(1)}, bf16[128,3584]{1,0:T(8,128)(2,1)S(1)}, u32[]{:S(2)}, u32[]{:S(2)}) collective-permute-start(bf16[128,3584]{1,0:T(8,128)(2,1)S(1)} %get-tuple-element.33), channel_id=1, source_target_pairs={{0,4},{12,8},{1,5},{13,9},{2,6},{14,10},{3,7},{15,11},{16,20},{28,... | collective-permute-start | bytes 2752520 | tf_op jit(solution)/shard_map/ppermute | solution.py:20
  370.8 18.1 %collective-permute-done.29 = bf16[128,3584]{1,0:T(8,128)(2,1)S(1)} collective-permute-done((bf16[128,3584]{1,0:T(8,128)(2,1)S(1)}, bf16[128,3584]{1,0:T(8,128)(2,1)S(1)}, u32[]{:S(2)}, u32[]{:S(2)}) %collective-permute-start.29) | collective-permute-done | bytes 917536 | tf_op jit(solution)/shard_map/ppermute | solution.py:20
  388.9 15.7 %collective-permute-done.32 = bf16[128,3584]{1,0:T(8,128)(2,1)S(1)} collective-permute-done((bf16[128,3584]{1,0:T(8,128)(2,1)S(1)}, bf16[128,3584]{1,0:T(8,128)(2,1)S(1)}, u32[]{:S(2)}, u32[]{:S(2)}) %collective-permute-start.32) | collective-permute-done | bytes 917536 | tf_op jit(solution)/shard_map/ppermute | solution.py:20
  411.6 59.2 %collective-permute-done.31 = bf16[128,3584]{1,0:T(8,128)(2,1)S(1)} collective-permute-done((bf16[128,3584]{1,0:T(8,128)(2,1)S(1)}, bf16[128,3584]{1,0:T(8,128)(2,1)S(1)}, u32[]{:S(2)}, u32[]{:S(2)}) %collective-permute-start.31) | collective-permute-done | bytes 917536 | tf_op jit(solution)/shard_map/ppermute | solution.py:26
  470.9 14.0 %collective-permute-done.34 = bf16[128,3584]{1,0:T(8,128)(2,1)S(1)} collective-permute-done((bf16[128,3584]{1,0:T(8,128)(2,1)S(1)}, bf16[128,3584]{1,0:T(8,128)(2,1)S(1)}, u32[]{:S(2)}, u32[]{:S(2)}) %collective-permute-start.34) | collective-permute-done | bytes 917536 | tf_op jit(solution)/shard_map/ppermute | solution.py:26
  486.4 3.6 broadcast_select_fusion.1
  490.0 27.8 %multiply_reduce_fusion = f32[1024,3584]{1,0:T(8,128)} fusion(bf16[4,128,3584]{2,1,0:T(8,128)(2,1)} %get-tuple-element.6, bf16[4,128,3584]{2,1,0:T(8,128)(2,1)} %get-tuple-element.5, bf16[4,128,1024]{1,2,0:T(8,128)(2,1)S(1)} %get-tuple-element.36, bf16[4,128,1024]{1,2,0:T(8,128)(2,1)S(1)} %get-tuple-element.35), kind=kOutput, calls=%fused_computation | convolution fusion | flops 7575961600 | bytes 24117248 | tf_op jit(solution)/shard_map/etd,etf->edf/dot_general | solution.py:95
  517.8 12.2 %broadcast_multiply_fusion = f32[1024,3584]{1,0:T(8,128)} fusion(f32[1024,3584]{1,0:T(8,128)} %multiply_reduce_fusion), kind=kLoop, calls=%fused_computation.4 | loop fusion | flops 3670016 | bytes 29360128 | tf_op jit(solution)/shard_map/div | solution.py:97
  (100 shorter events, 60.6 us)
Async XLA Ops:
  22.8 25.7 %collective-permute-start.8 = (bf16[128,3584]{1,0:T(8,128)(2,1)S(1)}, bf16[128,3584]{1,0:T(8,128)(2,1)S(1)}, u32[]{:S(2)}, u32[]{:S(2)}) collective-permute-start(bf16[128,3584]{1,0:T(8,128)(2,1)S(1)} %get-tuple-element.13), channel_id=1, source_target_pairs={{0,4},{12,8},{1,5},{13,9},{2,6},{14,10},{3,7},{15,11},{16,20},{28,... | collective-permute-start | bytes 2752520 | tf_op jit(solution)/shard_map/ppermute | solution.py:20
  27.8 40.3 %collective-permute-start.11 = (bf16[128,3584]{1,0:T(8,128)(2,1)S(1)}, bf16[128,3584]{1,0:T(8,128)(2,1)S(1)}, u32[]{:S(2)}, u32[]{:S(2)}) collective-permute-start(bf16[128,3584]{1,0:T(8,128)(2,1)S(1)} %get-tuple-element.14), channel_id=1, source_target_pairs={{0,4},{12,8},{1,5},{13,9},{2,6},{14,10},{3,7},{15,11},{16,20},{28,... | collective-permute-start | bytes 2752520 | tf_op jit(solution)/shard_map/ppermute | solution.py:20
  29.2 43.9 %collective-permute-start.1 = (bf16[4,32,4096]{2,1,0:T(8,128)(2,1)}, bf16[4,32,4096]{2,1,0:T(8,128)(2,1)S(1)}, u32[]{:S(2)}, u32[]{:S(2)}) collective-permute-start(bf16[4,32,4096]{2,1,0:T(8,128)(2,1)} %param.4), channel_id=1, source_target_pairs={{4,0},{8,4},{12,8},{5,1},{9,5},{13,9},{6,2},{10,6},{14,10},{7,3},{... | collective-permute-start | bytes 3145736 | tf_op jit(solution)/shard_map/ppermute | solution.py:38
  30.5 59.1 %collective-permute-start = (bf16[4,32,4096]{2,1,0:T(8,128)(2,1)}, bf16[4,32,4096]{2,1,0:T(8,128)(2,1)}, u32[]{:S(2)}, u32[]{:S(2)}) collective-permute-start(bf16[4,32,4096]{2,1,0:T(8,128)(2,1)} %param.4), channel_id=1, source_target_pairs={{0,4},{4,8},{8,12},{1,5},{5,9},{9,13},{2,6},{6,10},{10,14},{3,7},{... | collective-permute-start | bytes 3145736 | tf_op jit(solution)/shard_map/ppermute | solution.py:37
  69.9 21.0 %collective-permute-start.9 = (bf16[128,3584]{1,0:T(8,128)(2,1)}, bf16[128,3584]{1,0:T(8,128)(2,1)}, u32[]{:S(2)}, u32[]{:S(2)}) collective-permute-start(bf16[128,3584]{1,0:T(8,128)(2,1)} %get-tuple-element.11), channel_id=1, source_target_pairs={{4,8},{8,4},{5,9},{9,5},{6,10},{10,6},{7,11},{11,7},{20,24},{24,20... | collective-permute-start | bytes 2752520 | tf_op jit(solution)/shard_map/ppermute | solution.py:22
  71.5 28.4 %collective-permute-start.12 = (bf16[128,3584]{1,0:T(8,128)(2,1)}, bf16[128,3584]{1,0:T(8,128)(2,1)}, u32[]{:S(2)}, u32[]{:S(2)}) collective-permute-start(bf16[128,3584]{1,0:T(8,128)(2,1)} %get-tuple-element.12), channel_id=1, source_target_pairs={{4,8},{8,4},{5,9},{9,5},{6,10},{10,6},{7,11},{11,7},{20,24},{24,20... | collective-permute-start | bytes 2752520 | tf_op jit(solution)/shard_map/ppermute | solution.py:22
  73.1 114.0 %collective-permute-start.21 = (bf16[4,64,7168]{2,1,0:T(8,128)(2,1)}, bf16[4,64,7168]{2,1,0:T(8,128)(2,1)}, u32[]{:S(2)}, u32[]{:S(2)}) collective-permute-start(bf16[4,64,7168]{2,1,0:T(8,128)(2,1)} %param.5), channel_id=1, source_target_pairs={{0,1},{1,0},{2,3},{3,2},{4,5},{5,4},{6,7},{7,6},{8,9},{9,8},{10,11... | collective-permute-start | bytes 11010056 | tf_op jit(solution)/shard_map/ppermute | solution.py:48
  73.1 144.2 %collective-permute-start.14 = (bf16[4,64,7168]{2,1,0:T(8,128)(2,1)}, bf16[4,64,7168]{2,1,0:T(8,128)(2,1)}, u32[]{:S(2)}, u32[]{:S(2)}) collective-permute-start(bf16[4,64,7168]{2,1,0:T(8,128)(2,1)} %param.5), channel_id=1, source_target_pairs={{0,2},{2,0},{1,3},{3,1},{4,6},{6,4},{5,7},{7,5},{8,10},{10,8},{9,1... | collective-permute-start | bytes 11010056 | tf_op jit(solution)/shard_map/ppermute | solution.py:66
  89.6 26.7 %collective-permute-start.2 = (bf16[4,32,4096]{2,1,0:T(8,128)(2,1)S(1)}, bf16[4,32,4096]{2,1,0:T(8,128)(2,1)S(1)}, u32[]{:S(2)}, u32[]{:S(2)}) collective-permute-start(bf16[4,32,4096]{2,1,0:T(8,128)(2,1)S(1)} %collective-permute-done.1), channel_id=1, source_target_pairs={{4,0},{8,4},{12,8},{5,1},{9,5},{13,9},{6,2},{10,6},{14,10},{7,3},{... | collective-permute-start | bytes 3145736 | tf_op jit(solution)/shard_map/ppermute | solution.py:38
  90.9 26.9 %collective-permute-start.4 = (bf16[4,32,4096]{2,1,0:T(8,128)(2,1)}, bf16[4,32,4096]{2,1,0:T(8,128)(2,1)S(1)}, u32[]{:S(2)}, u32[]{:S(2)}) collective-permute-start(bf16[4,32,4096]{2,1,0:T(8,128)(2,1)} %collective-permute-done), channel_id=1, source_target_pairs={{0,4},{4,8},{8,12},{1,5},{5,9},{9,13},{2,6},{6,10},{10,14},{3,7},{... | collective-permute-start | bytes 3145736 | tf_op jit(solution)/shard_map/ppermute | solution.py:37
  103.1 33.5 %collective-permute-start.10 = (bf16[128,3584]{1,0:T(8,128)(2,1)S(1)}, bf16[128,3584]{1,0:T(8,128)(2,1)S(1)}, u32[]{:S(2)}, u32[]{:S(2)}) collective-permute-start(bf16[128,3584]{1,0:T(8,128)(2,1)S(1)} %get-tuple-element.9), channel_id=1, source_target_pairs={{4,0},{8,12},{5,1},{9,13},{6,2},{10,14},{7,3},{11,15},{20,16},{24,... | collective-permute-start | bytes 2752520 | tf_op jit(solution)/shard_map/ppermute | solution.py:26
  116.3 43.0 %collective-permute-start.13 = (bf16[128,3584]{1,0:T(8,128)(2,1)S(1)}, bf16[128,3584]{1,0:T(8,128)(2,1)S(1)}, u32[]{:S(2)}, u32[]{:S(2)}) collective-permute-start(bf16[128,3584]{1,0:T(8,128)(2,1)S(1)} %get-tuple-element.10), channel_id=1, source_target_pairs={{4,0},{8,12},{5,1},{9,13},{6,2},{10,14},{7,3},{11,15},{20,16},{24,... | collective-permute-start | bytes 2752520 | tf_op jit(solution)/shard_map/ppermute | solution.py:26
  117.8 60.6 %collective-permute-start.3 = (bf16[4,32,4096]{2,1,0:T(8,128)(2,1)S(1)}, bf16[4,32,4096]{2,1,0:T(8,128)(2,1)S(1)}, u32[]{:S(2)}, u32[]{:S(2)}) collective-permute-start(bf16[4,32,4096]{2,1,0:T(8,128)(2,1)S(1)} %collective-permute-done.2), channel_id=1, source_target_pairs={{4,0},{8,4},{12,8},{5,1},{9,5},{13,9},{6,2},{10,6},{14,10},{7,3},{... | collective-permute-start | bytes 3145736 | tf_op jit(solution)/shard_map/ppermute | solution.py:38
  136.6 41.9 %collective-permute-start.5 = (bf16[4,32,4096]{2,1,0:T(8,128)(2,1)S(1)}, bf16[4,32,4096]{2,1,0:T(8,128)(2,1)S(1)}, u32[]{:S(2)}, u32[]{:S(2)}) collective-permute-start(bf16[4,32,4096]{2,1,0:T(8,128)(2,1)S(1)} %collective-permute-done.4), channel_id=1, source_target_pairs={{0,4},{4,8},{8,12},{1,5},{5,9},{9,13},{2,6},{6,10},{10,14},{3,7},{... | collective-permute-start | bytes 3145736 | tf_op jit(solution)/shard_map/ppermute | solution.py:37
  185.6 60.8 %collective-permute-start.6 = (bf16[512,1024]{1,0:T(8,128)(2,1)S(1)}, bf16[512,1024]{1,0:T(8,128)(2,1)S(1)}, u32[]{:S(2)}, u32[]{:S(2)}) collective-permute-start(bf16[512,1024]{1,0:T(8,128)(2,1)S(1)} %get-tuple-element.45), channel_id=1, source_target_pairs={{0,2},{2,0},{1,3},{3,1},{4,6},{6,4},{5,7},{7,5},{8,10},{10,8},{9,1... | collective-permute-start | bytes 3145736 | tf_op jit(solution)/shard_map/ppermute | solution.py:86
  211.5 42.9 %collective-permute-start.22 = (bf16[128,3584]{1,0:T(8,128)(2,1)}, bf16[128,3584]{1,0:T(8,128)(2,1)}, u32[]{:S(2)}, u32[]{:S(2)}) collective-permute-start(bf16[128,3584]{1,0:T(8,128)(2,1)} %get-tuple-element.27), channel_id=1, source_target_pairs={{0,4},{12,8},{1,5},{13,9},{2,6},{14,10},{3,7},{15,11},{16,20},{28,... | collective-permute-start | bytes 2752520 | tf_op jit(solution)/shard_map/ppermute | solution.py:20
  215.1 39.9 %collective-permute-start.25 = (bf16[128,3584]{1,0:T(8,128)(2,1)}, bf16[128,3584]{1,0:T(8,128)(2,1)}, u32[]{:S(2)}, u32[]{:S(2)}) collective-permute-start(bf16[128,3584]{1,0:T(8,128)(2,1)} %get-tuple-element.28), channel_id=1, source_target_pairs={{0,4},{12,8},{1,5},{13,9},{2,6},{14,10},{3,7},{15,11},{16,20},{28,... | collective-permute-start | bytes 2752520 | tf_op jit(solution)/shard_map/ppermute | solution.py:20
  241.7 32.8 %collective-permute-start.15 = (bf16[128,3584]{1,0:T(8,128)(2,1)}, bf16[128,3584]{1,0:T(8,128)(2,1)}, u32[]{:S(2)}, u32[]{:S(2)}) collective-permute-start(bf16[128,3584]{1,0:T(8,128)(2,1)} %get-tuple-element.19), channel_id=1, source_target_pairs={{0,4},{12,8},{1,5},{13,9},{2,6},{14,10},{3,7},{15,11},{16,20},{28,... | collective-permute-start | bytes 2752520 | tf_op jit(solution)/shard_map/ppermute | solution.py:20
  244.0 45.7 %collective-permute-start.18 = (bf16[128,3584]{1,0:T(8,128)(2,1)}, bf16[128,3584]{1,0:T(8,128)(2,1)}, u32[]{:S(2)}, u32[]{:S(2)}) collective-permute-start(bf16[128,3584]{1,0:T(8,128)(2,1)} %get-tuple-element.20), channel_id=1, source_target_pairs={{0,4},{12,8},{1,5},{13,9},{2,6},{14,10},{3,7},{15,11},{16,20},{28,... | collective-permute-start | bytes 2752520 | tf_op jit(solution)/shard_map/ppermute | solution.py:20
  246.4 80.0 %collective-permute-start.28 = (bf16[4,64,7168]{2,1,0:T(8,128)(2,1)}, bf16[4,64,7168]{2,1,0:T(8,128)(2,1)}, u32[]{:S(2)}, u32[]{:S(2)}) collective-permute-start(bf16[4,64,7168]{2,1,0:T(8,128)(2,1)} %collective-permute-done.14), channel_id=1, source_target_pairs={{0,1},{1,0},{2,3},{3,2},{4,5},{5,4},{6,7},{7,6},{8,9},{9,8},{10,11... | collective-permute-start | bytes 11010056 | tf_op jit(solution)/shard_map/ppermute | solution.py:48
  254.4 38.0 %collective-permute-start.7 = (bf16[4,128,1024]{1,2,0:T(8,128)(2,1)S(1)}, bf16[4,128,1024]{1,2,0:T(8,128)(2,1)S(1)}, u32[]{:S(2)}, u32[]{:S(2)}) collective-permute-start(bf16[4,128,1024]{1,2,0:T(8,128)(2,1)S(1)} %pad_maximum_fusion.8), channel_id=1, source_target_pairs={{0,1},{1,0},{2,3},{3,2},{4,5},{5,4},{6,7},{7,6},{8,9},{9,8},{10,11... | collective-permute-start | bytes 3145736 | tf_op jit(solution)/shard_map/ppermute | solution.py:48
  257.2 36.0 %collective-permute-start.23 = (bf16[128,3584]{1,0:T(8,128)(2,1)S(1)}, bf16[128,3584]{1,0:T(8,128)(2,1)S(1)}, u32[]{:S(2)}, u32[]{:S(2)}) collective-permute-start(bf16[128,3584]{1,0:T(8,128)(2,1)S(1)} %get-tuple-element.25), channel_id=1, source_target_pairs={{4,8},{8,4},{5,9},{9,5},{6,10},{10,6},{7,11},{11,7},{20,24},{24,20... | collective-permute-start | bytes 2752520 | tf_op jit(solution)/shard_map/ppermute | solution.py:22
  274.6 18.7 %collective-permute-start.26 = (bf16[128,3584]{1,0:T(8,128)(2,1)S(1)}, bf16[128,3584]{1,0:T(8,128)(2,1)S(1)}, u32[]{:S(2)}, u32[]{:S(2)}) collective-permute-start(bf16[128,3584]{1,0:T(8,128)(2,1)S(1)} %get-tuple-element.26), channel_id=1, source_target_pairs={{4,8},{8,4},{5,9},{9,5},{6,10},{10,6},{7,11},{11,7},{20,24},{24,20... | collective-permute-start | bytes 2752520 | tf_op jit(solution)/shard_map/ppermute | solution.py:22
  291.6 6.4 %collective-permute-start.16 = (bf16[128,3584]{1,0:T(8,128)(2,1)S(1)}, bf16[128,3584]{1,0:T(8,128)(2,1)S(1)}, u32[]{:S(2)}, u32[]{:S(2)}) collective-permute-start(bf16[128,3584]{1,0:T(8,128)(2,1)S(1)} %get-tuple-element.17), channel_id=1, source_target_pairs={{4,8},{8,4},{5,9},{9,5},{6,10},{10,6},{7,11},{11,7},{20,24},{24,20... | collective-permute-start | bytes 2752520 | tf_op jit(solution)/shard_map/ppermute | solution.py:22
  295.5 30.8 %collective-permute-start.24 = (bf16[128,3584]{1,0:T(8,128)(2,1)S(1)}, bf16[128,3584]{1,0:T(8,128)(2,1)S(1)}, u32[]{:S(2)}, u32[]{:S(2)}) collective-permute-start(bf16[128,3584]{1,0:T(8,128)(2,1)S(1)} %get-tuple-element.23), channel_id=1, source_target_pairs={{4,0},{8,12},{5,1},{9,13},{6,2},{10,14},{7,3},{11,15},{20,16},{24,... | collective-permute-start | bytes 2752520 | tf_op jit(solution)/shard_map/ppermute | solution.py:26
  296.8 72.7 %collective-permute-start.27 = (bf16[128,3584]{1,0:T(8,128)(2,1)S(1)}, bf16[128,3584]{1,0:T(8,128)(2,1)}, u32[]{:S(2)}, u32[]{:S(2)}) collective-permute-start(bf16[128,3584]{1,0:T(8,128)(2,1)S(1)} %get-tuple-element.24), channel_id=1, source_target_pairs={{4,0},{8,12},{5,1},{9,13},{6,2},{10,14},{7,3},{11,15},{20,16},{24,... | collective-permute-start | bytes 2752520 | tf_op jit(solution)/shard_map/ppermute | solution.py:26
  300.3 106.4 %collective-permute-start.17 = (bf16[128,3584]{1,0:T(8,128)(2,1)S(1)}, bf16[128,3584]{1,0:T(8,128)(2,1)}, u32[]{:S(2)}, u32[]{:S(2)}) collective-permute-start(bf16[128,3584]{1,0:T(8,128)(2,1)S(1)} %get-tuple-element.15), channel_id=1, source_target_pairs={{4,0},{8,12},{5,1},{9,13},{6,2},{10,14},{7,3},{11,15},{20,16},{24,... | collective-permute-start | bytes 2752520 | tf_op jit(solution)/shard_map/ppermute | solution.py:26
  301.6 108.5 %collective-permute-start.20 = (bf16[128,3584]{1,0:T(8,128)(2,1)S(1)}, bf16[128,3584]{1,0:T(8,128)(2,1)S(1)}, u32[]{:S(2)}, u32[]{:S(2)}) collective-permute-start(bf16[128,3584]{1,0:T(8,128)(2,1)S(1)} %get-tuple-element.16), channel_id=1, source_target_pairs={{4,0},{8,12},{5,1},{9,13},{6,2},{10,14},{7,3},{11,15},{20,16},{24,... | collective-permute-start | bytes 2752520 | tf_op jit(solution)/shard_map/ppermute | solution.py:26
  349.3 39.5 %collective-permute-start.29 = (bf16[128,3584]{1,0:T(8,128)(2,1)S(1)}, bf16[128,3584]{1,0:T(8,128)(2,1)S(1)}, u32[]{:S(2)}, u32[]{:S(2)}) collective-permute-start(bf16[128,3584]{1,0:T(8,128)(2,1)S(1)} %get-tuple-element.33), channel_id=1, source_target_pairs={{0,4},{12,8},{1,5},{13,9},{2,6},{14,10},{3,7},{15,11},{16,20},{28,... | collective-permute-start | bytes 2752520 | tf_op jit(solution)/shard_map/ppermute | solution.py:20
  368.1 36.4 %collective-permute-start.32 = (bf16[128,3584]{1,0:T(8,128)(2,1)S(1)}, bf16[128,3584]{1,0:T(8,128)(2,1)S(1)}, u32[]{:S(2)}, u32[]{:S(2)}) collective-permute-start(bf16[128,3584]{1,0:T(8,128)(2,1)S(1)} %get-tuple-element.34), channel_id=1, source_target_pairs={{0,4},{12,8},{1,5},{13,9},{2,6},{14,10},{3,7},{15,11},{16,20},{28,... | collective-permute-start | bytes 2752520 | tf_op jit(solution)/shard_map/ppermute | solution.py:20
  408.7 62.0 %collective-permute-start.31 = (bf16[128,3584]{1,0:T(8,128)(2,1)S(1)}, bf16[128,3584]{1,0:T(8,128)(2,1)S(1)}, u32[]{:S(2)}, u32[]{:S(2)}) collective-permute-start(bf16[128,3584]{1,0:T(8,128)(2,1)S(1)} %get-tuple-element.29), channel_id=1, source_target_pairs={{4,0},{8,12},{5,1},{9,13},{6,2},{10,14},{7,3},{11,15},{20,16},{24,... | collective-permute-start | bytes 2752520 | tf_op jit(solution)/shard_map/ppermute | solution.py:26
  410.3 74.6 %collective-permute-start.34 = (bf16[128,3584]{1,0:T(8,128)(2,1)S(1)}, bf16[128,3584]{1,0:T(8,128)(2,1)S(1)}, u32[]{:S(2)}, u32[]{:S(2)}) collective-permute-start(bf16[128,3584]{1,0:T(8,128)(2,1)S(1)} %get-tuple-element.30), channel_id=1, source_target_pairs={{4,0},{8,12},{5,1},{9,13},{6,2},{10,14},{7,3},{11,15},{20,16},{24,... | collective-permute-start | bytes 2752520 | tf_op jit(solution)/shard_map/ppermute | solution.py:26
  (12 other events, 287.4 us)

commit v2 on v1

--- a/solution.py
+++ b/solution.py
@@ -67,17 +67,16 @@
         acts = jnp.stack(gather_on_line(activations, "out", n_out))
 
         def project(block):
+            block = lax.all_gather(block, "dp", axis=0, tiled=True)
             e, t, f = block.shape
             partial = jnp.dot(block.reshape(e * t, f), basis_out, preferred_element_type=F32)
-            cuts = 2 if e % 2 == 0 and (e // 2) * t % 16 == 0 else 1
+            cuts = 4 if e % 4 == 0 and (e // 4) * t % 16 == 0 else 1
             rows = e * t // cuts
-            sums = [sum_on_line(partial[c * rows:(c + 1) * rows], "out", n_out) for c in range(cuts)]
+            parts = [lax.optimization_barrier(partial[c * rows:(c + 1) * rows]) for c in range(cuts)]
+            sums = [sum_on_line(part, "out", n_out) for part in parts]
             return jnp.concatenate(sums, axis=0).reshape(e, t, -1)
 
-        mine, others = [], []
-        for block in grads:
-            mine.append(project(block))
-            others.append(project(swap_dp(block)))
+        projected = [project(block) for block in grads]
 
         act_partial = jnp.dot(acts.reshape(n_out * ex * tok, width), basis_in, preferred_element_type=F32)
         total = act_partial
@@ -86,15 +85,20 @@
             total = total + lax.ppermute(sent, "inp", [(i, (i + k) % n_inp) for i in range(n_inp)]).astype(F32)
         act_own = total.astype(BF16).reshape(n_out, ex, tok, -1)
         act_own = jnp.concatenate(in_order([act_own[k] for k in range(n_out)], "out", n_out), axis=1)
+        count_rows = n_dp * act_own.shape[0] * act_own.shape[1]
+        root = 1
+        while root * root < count_rows:
+            root *= 2
+        scaled = root * root == count_rows
+        if scaled:
+            act_own = act_own * jnp.asarray(1.0 / root, BF16)
         act_hat = by_dp(act_own, swap_dp(act_own))
 
-        grad_mine = jnp.concatenate(in_order(mine, "inp", n_inp), axis=1)
-        grad_others = jnp.concatenate(in_order(others, "inp", n_inp), axis=1)
-        grad_hat = by_dp(grad_mine, grad_others)
+        grad_hat = jnp.concatenate(in_order(projected, "inp", n_inp), axis=1)
 
         rotated = jnp.einsum("etd,etf->edf", act_hat, grad_hat, preferred_element_type=F32)
-        count_rows = act_hat.shape[0] * act_hat.shape[1]
-        return jnp.sum(rotated * rotated, axis=0) / count_rows
+        total = jnp.sum(rotated * rotated, axis=0)
+        return total if scaled else total / count_rows
 
     return body
 

time: 537 us -> 545 us (1.015); the launches traced: 530 us -> 544 us
  waiting for transfers between devices: 272 us -> 344 us
  starting transfers between devices: 83 us -> 50.6 us
  matrix products: 123 us -> 98.4 us
  other arithmetic: 42.5 us -> 24.3 us
  between operations: 1.06 us -> 14.1 us
    ppermute x3, waiting for transfers between devices: 29.9 us -> 59.9 us  [gather_on_line(): lefts.append(lax.ppermute(lefts[-1], axis, down))]
    ppermute x1, waiting for transfers between devices: 0.01 us -> 25.9 us  [body(): lax.ppermute(out_grads, 'inp', [(i, (i + k) % n_inp) for i in range(n_inp)])]
    dot_general x4 -> x2, matrix products: 90.7 us -> 65.3 us  [project(): jnp.dot(block.reshape(e * t, f), basis_out, preferred_element_type=F32)]
    ppermute x1, waiting for transfers between devices: 0.01 us -> 24.3 us  [body(): lax.ppermute(sent, 'inp', [(i, (i + k) % n_inp) for i in range(n_inp)])]
    ppermute x8, starting transfers between devices: 37 us -> 13.5 us  [sum_on_line(): total = total + lax.ppermute(total.astype(BF16), axis, hops).astype(F32)]
    ppermute x3, waiting for transfers between devices: 15.2 us -> 0.01 us  [gather_on_line(): rights.append(lax.ppermute(rights[-1], axis, up))]
    div x1 -> x0, other arithmetic: 12.2 us -> none  [body(): return jnp.sum(rotated * rotated, axis=0) / count_rows]
    ppermute x8, waiting for transfers between devices: 96.8 us -> 108 us  [sum_on_line(): total = total + lax.ppermute(total.astype(BF16), axis, hops).astype(F32)]
  transfers between devices with their start and end apart: 35 -> 35, of which waited for: 15 -> 19; matrix products, arithmetic and copies ran while one was open for 20% -> 18% of each run, Pallas kernels for 0% -> 0%
where the time goes in v2:
time: 545 us; the launch traced here: 544 us
  waiting for transfers between devices  344 us (63%)
  matrix products  98.4 us (18%)
  starting transfers between devices  50.6 us (9%)
  other arithmetic  24.3 us (4%)
  between operations  14.1 us (3%)
  local copies, waits for them, and re-layouts  12.6 us (2%)
    ppermute x8, waiting for transfers between devices, sum_on_line(): got = lax.ppermute(out, axis, hops)  126 us
    ppermute x8, waiting for transfers between devices, sum_on_line(): total = total + lax.ppermute(total.astype(BF16), axis, hops).astype(F32)  108 us
    dot_general x2, matrix products, project(): jnp.dot(block.reshape(e * t, f), basis_out, preferred_element_type=F32)  65.3 us
    ppermute x3, waiting for transfers between devices, gather_on_line(): lefts.append(lax.ppermute(lefts[-1], axis, down))  59.9 us
    dot_general x1, matrix products, body(): jnp.einsum('etd,etf->edf', act_hat, grad_hat, preferred_element_type=F32)  27.7 us
    ppermute x1, waiting for transfers between devices, body(): lax.ppermute(out_grads, 'inp', [(i, (i + k) % n_inp) for i in range(n_inp)])  25.9 us
    ppermute x1, waiting for transfers between devices, body(): lax.ppermute(sent, 'inp', [(i, (i + k) % n_inp) for i in range(n_inp)])  24.3 us
    ppermute x3, starting transfers between devices, gather_on_line(): rights.append(lax.ppermute(rights[-1], axis, up))  14.9 us
  transfers between devices with their start and end apart: 35, of which 19 were waited for; matrix products, arithmetic and copies ran while one was open for 18% of the time, Pallas kernels for 0%

profile of v2, /device:TPU:0, one launch (start us, length us, event | category | flops | bytes accessed | tf_op | source)
XLA Modules:
  0.0 544.1 jit_solution(1049700828327189148)
XLA Ops:
  7.8 5.6 %collective-permute-start = (bf16[4,32,4096]{2,1,0:T(8,128)(2,1)}, bf16[4,32,4096]{2,1,0:T(8,128)(2,1)S(1)}, u32[]{:S(2)}, u32[]{:S(2)}) collective-permute-start(bf16[4,32,4096]{2,1,0:T(8,128)(2,1)} %param.4), channel_id=1, source_target_pairs={{0,4},{4,8},{8,12},{1,5},{5,9},{9,13},{2,6},{6,10},{10,14},{3,7},{... | collective-permute-start | bytes 3145736 | tf_op jit(solution)/shard_map/ppermute | solution.py:37
  13.5 21.4 %collective-permute-done.1 = bf16[4,32,4096]{2,1,0:T(8,128)(2,1)S(1)} collective-permute-done((bf16[4,32,4096]{2,1,0:T(8,128)(2,1)}, bf16[4,32,4096]{2,1,0:T(8,128)(2,1)S(1)}, u32[]{:S(2)}, u32[]{:S(2)}) %collective-permute-start.1) | collective-permute-done | bytes 1048608 | tf_op jit(solution)/shard_map/ppermute | solution.py:38
  36.1 4.6 collective-permute-start.4
  40.8 20.3 %collective-permute-done.2 = bf16[4,32,4096]{2,1,0:T(8,128)(2,1)} collective-permute-done((bf16[4,32,4096]{2,1,0:T(8,128)(2,1)S(1)}, bf16[4,32,4096]{2,1,0:T(8,128)(2,1)}, u32[]{:S(2)}, u32[]{:S(2)}) %collective-permute-start.2) | collective-permute-done | bytes 1048608 | tf_op jit(solution)/shard_map/ppermute | solution.py:38
  62.5 4.6 collective-permute-start.5
  68.6 18.2 %collective-permute-done.3 = bf16[4,32,4096]{2,1,0:T(8,128)(2,1)} collective-permute-done((bf16[4,32,4096]{2,1,0:T(8,128)(2,1)}, bf16[4,32,4096]{2,1,0:T(8,128)(2,1)}, u32[]{:S(2)}, u32[]{:S(2)}) %collective-permute-start.3) | collective-permute-done | bytes 1048608 | tf_op jit(solution)/shard_map/ppermute | solution.py:38
  90.6 5.5 %fusion.18 = (bf16[512,1024]{1,0:T(8,128)(2,1)}, f32[512,1024]{1,0:T(8,128)S(1)}) fusion(bf16[512,4096]{1,0:T(8,128)(2,1)S(1)} %bitcast.30, bf16[4096,1024]{1,0:T(8,128)(2,1)S(1)} %bitcast.39), kind=kOutput, calls=%fused_computation.60 | convolution fusion | flops 4295491584 | bytes 15728640 | tf_op jit(solution)/shard_map/dot_general | solution.py:81
  98.1 24.3 %collective-permute-done.6 = bf16[512,1024]{1,0:T(8,128)(2,1)S(1)} collective-permute-done((bf16[512,1024]{1,0:T(8,128)(2,1)}, bf16[512,1024]{1,0:T(8,128)(2,1)S(1)}, u32[]{:S(2)}, u32[]{:S(2)}) %collective-permute-start.6) | collective-permute-done | bytes 1048608 | tf_op jit(solution)/shard_map/ppermute | solution.py:85
  127.6 3.3 maximum_multiply_fusion
  131.0 32.7 %fusion.19 = f32[512,3584]{1,0:T(8,128)S(1)} fusion(bf16[512,7168]{1,0:T(8,128)(2,1)} %bitcast.40, bf16[7168,3584]{1,0:T(8,128)(2,1)} %param.7), kind=kOutput, calls=%fused_computation.61 | convolution fusion | flops 26306674688 | bytes 66060288 | tf_op jit(solution)/shard_map/dot_general | solution.py:72
  163.6 2.5 fusion.15
  168.5 3.1 collective-permute-start.11
  171.6 25.9 %collective-permute-done.20 = bf16[4,64,7168]{2,1,0:T(8,128)(2,1)} collective-permute-done((bf16[4,64,7168]{2,1,0:T(8,128)(2,1)}, bf16[4,64,7168]{2,1,0:T(8,128)(2,1)}, u32[]{:S(2)}, u32[]{:S(2)}) %collective-permute-start.20) | collective-permute-done | bytes 3670048 | tf_op jit(solution)/shard_map/ppermute | solution.py:66
  197.6 2.7 broadcast_select_fusion.3
  202.4 2.1 collective-permute-start.14
  209.5 15.7 %collective-permute-done.14 = bf16[128,3584]{1,0:T(8,128)(2,1)S(1)} collective-permute-done((bf16[128,3584]{1,0:T(8,128)(2,1)S(1)}, bf16[128,3584]{1,0:T(8,128)(2,1)S(1)}, u32[]{:S(2)}, u32[]{:S(2)}) %collective-permute-start.14) | collective-permute-done | bytes 917536 | tf_op jit(solution)/shard_map/ppermute | solution.py:20
  226.1 18.8 %collective-permute-done.8 = bf16[128,3584]{1,0:T(8,128)(2,1)S(1)} collective-permute-done((bf16[128,3584]{1,0:T(8,128)(2,1)S(1)}, bf16[128,3584]{1,0:T(8,128)(2,1)S(1)}, u32[]{:S(2)}, u32[]{:S(2)}) %collective-permute-start.8) | collective-permute-done | bytes 917536 | tf_op jit(solution)/shard_map/ppermute | solution.py:20
  245.8 14.1 %collective-permute-done.17 = bf16[128,3584]{1,0:T(8,128)(2,1)S(1)} collective-permute-done((bf16[128,3584]{1,0:T(8,128)(2,1)S(1)}, bf16[128,3584]{1,0:T(8,128)(2,1)S(1)}, u32[]{:S(2)}, u32[]{:S(2)}) %collective-permute-start.17) | collective-permute-done | bytes 917536 | tf_op jit(solution)/shard_map/ppermute | solution.py:20
  269.3 20.1 %collective-permute-done.13 = bf16[128,3584]{1,0:T(8,128)(2,1)S(1)} collective-permute-done((bf16[128,3584]{1,0:T(8,128)(2,1)S(1)}, bf16[128,3584]{1,0:T(8,128)(2,1)S(1)}, u32[]{:S(2)}, u32[]{:S(2)}) %collective-permute-start.13) | collective-permute-done | bytes 917536 | tf_op jit(solution)/shard_map/ppermute | solution.py:26
  289.5 19.6 %collective-permute-done.16 = bf16[128,3584]{1,0:T(8,128)(2,1)S(1)} collective-permute-done((bf16[128,3584]{1,0:T(8,128)(2,1)S(1)}, bf16[128,3584]{1,0:T(8,128)(2,1)S(1)}, u32[]{:S(2)}, u32[]{:S(2)}) %collective-permute-start.16) | collective-permute-done | bytes 917536 | tf_op jit(solution)/shard_map/ppermute | solution.py:26
  309.1 19.6 %collective-permute-done.10 = bf16[128,3584]{1,0:T(8,128)(2,1)S(1)} collective-permute-done((bf16[128,3584]{1,0:T(8,128)(2,1)S(1)}, bf16[128,3584]{1,0:T(8,128)(2,1)S(1)}, u32[]{:S(2)}, u32[]{:S(2)}) %collective-permute-start.10) | collective-permute-done | bytes 917536 | tf_op jit(solution)/shard_map/ppermute | solution.py:26
  328.8 32.7 %fusion.20 = f32[512,3584]{1,0:T(8,128)S(1)} fusion(bf16[512,7168]{1,0:T(8,128)(2,1)} %bitcast.41, bf16[7168,3584]{1,0:T(8,128)(2,1)} %param.7), kind=kOutput, calls=%fused_computation.62 | convolution fusion | flops 26306674688 | bytes 66060288 | tf_op jit(solution)/shard_map/dot_general | solution.py:72
  369.3 15.1 %collective-permute-done.24 = bf16[128,3584]{1,0:T(8,128)(2,1)S(1)} collective-permute-done((bf16[128,3584]{1,0:T(8,128)(2,1)S(1)}, bf16[128,3584]{1,0:T(8,128)(2,1)S(1)}, u32[]{:S(2)}, u32[]{:S(2)}) %collective-permute-start.24) | collective-permute-done | bytes 917536 | tf_op jit(solution)/shard_map/ppermute | solution.py:20
  385.2 18.8 %collective-permute-done.27 = bf16[128,3584]{1,0:T(8,128)(2,1)S(1)} collective-permute-done((bf16[128,3584]{1,0:T(8,128)(2,1)S(1)}, bf16[128,3584]{1,0:T(8,128)(2,1)S(1)}, u32[]{:S(2)}, u32[]{:S(2)}) %collective-permute-start.27) | collective-permute-done | bytes 917536 | tf_op jit(solution)/shard_map/ppermute | solution.py:20
  404.9 16.3 %collective-permute-done.21 = bf16[128,3584]{1,0:T(8,128)(2,1)S(1)} collective-permute-done((bf16[128,3584]{1,0:T(8,128)(2,1)S(1)}, bf16[128,3584]{1,0:T(8,128)(2,1)S(1)}, u32[]{:S(2)}, u32[]{:S(2)}) %collective-permute-start.21) | collective-permute-done | bytes 917536 | tf_op jit(solution)/shard_map/ppermute | solution.py:20
  422.1 8.9 %collective-permute-done.30 = bf16[128,3584]{1,0:T(8,128)(2,1)S(1)} collective-permute-done((bf16[128,3584]{1,0:T(8,128)(2,1)S(1)}, bf16[128,3584]{1,0:T(8,128)(2,1)S(1)}, u32[]{:S(2)}, u32[]{:S(2)}) %collective-permute-start.30) | collective-permute-done | bytes 917536 | tf_op jit(solution)/shard_map/ppermute | solution.py:20
  438.5 21.3 %collective-permute-done.26 = bf16[128,3584]{1,0:T(8,128)(2,1)S(1)} collective-permute-done((bf16[128,3584]{1,0:T(8,128)(2,1)S(1)}, bf16[128,3584]{1,0:T(8,128)(2,1)S(1)}, u32[]{:S(2)}, u32[]{:S(2)}) %collective-permute-start.26) | collective-permute-done | bytes 917536 | tf_op jit(solution)/shard_map/ppermute | solution.py:26
  459.9 19.6 %collective-permute-done.29 = bf16[128,3584]{1,0:T(8,128)(2,1)S(1)} collective-permute-done((bf16[128,3584]{1,0:T(8,128)(2,1)S(1)}, bf16[128,3584]{1,0:T(8,128)(2,1)S(1)}, u32[]{:S(2)}, u32[]{:S(2)}) %collective-permute-start.29) | collective-permute-done | bytes 917536 | tf_op jit(solution)/shard_map/ppermute | solution.py:26
  479.6 16.4 %collective-permute-done.23 = bf16[128,3584]{1,0:T(8,128)(2,1)S(1)} collective-permute-done((bf16[128,3584]{1,0:T(8,128)(2,1)S(1)}, bf16[128,3584]{1,0:T(8,128)(2,1)S(1)}, u32[]{:S(2)}, u32[]{:S(2)}) %collective-permute-start.23) | collective-permute-done | bytes 917536 | tf_op jit(solution)/shard_map/ppermute | solution.py:26
  496.1 9.7 %collective-permute-done.32 = bf16[128,3584]{1,0:T(8,128)(2,1)S(1)} collective-permute-done((bf16[128,3584]{1,0:T(8,128)(2,1)S(1)}, bf16[128,3584]{1,0:T(8,128)(2,1)S(1)}, u32[]{:S(2)}, u32[]{:S(2)}) %collective-permute-start.32) | collective-permute-done | bytes 917536 | tf_op jit(solution)/shard_map/ppermute | solution.py:26
  506.0 3.6 broadcast_select_fusion.1
  509.6 27.7 %multiply_reduce_fusion = f32[1024,3584]{1,0:T(8,128)} fusion(bf16[8,64,3584]{2,1,0:T(8,128)(2,1)} %bitcast.32, bf16[8,64,3584]{2,1,0:T(8,128)(2,1)} %bitcast.31, bf16[4,128,1024]{1,2,0:T(8,128)(2,1)} %get-tuple-element.16, bf16[4,128,1024]{1,2,0:T(8,128)(2,1)} %get-tuple-element.15), kind=kOutput, calls=%fused_computation | convolution fusion | flops 7586971648 | bytes 24117248 | tf_op jit(solution)/shard_map/etd,etf->edf/dot_general | solution.py:99
  (108 shorter events, 55.5 us)
Async XLA Ops:
  6.5 124.4 %all-gather.3.cloned.1.call-start = ((), (), s32[]{:S(2)}) async-start(), calls=%async_computation | async-start | bytes 11010048 | tf_op jit(solution)/shard_map/all_gather | solution.py:70
  6.5 28.3 %collective-permute-start.1 = (bf16[4,32,4096]{2,1,0:T(8,128)(2,1)}, bf16[4,32,4096]{2,1,0:T(8,128)(2,1)S(1)}, u32[]{:S(2)}, u32[]{:S(2)}) collective-permute-start(bf16[4,32,4096]{2,1,0:T(8,128)(2,1)} %param.4), channel_id=1, source_target_pairs={{4,0},{8,4},{12,8},{5,1},{9,5},{13,9},{6,2},{10,6},{14,10},{7,3},{... | collective-permute-start | bytes 3145736 | tf_op jit(solution)/shard_map/ppermute | solution.py:38
  7.8 28.3 %collective-permute-start = (bf16[4,32,4096]{2,1,0:T(8,128)(2,1)}, bf16[4,32,4096]{2,1,0:T(8,128)(2,1)S(1)}, u32[]{:S(2)}, u32[]{:S(2)}) collective-permute-start(bf16[4,32,4096]{2,1,0:T(8,128)(2,1)} %param.4), channel_id=1, source_target_pairs={{0,4},{4,8},{8,12},{1,5},{5,9},{9,13},{2,6},{6,10},{10,14},{3,7},{... | collective-permute-start | bytes 3145736 | tf_op jit(solution)/shard_map/ppermute | solution.py:37
  34.8 26.3 %collective-permute-start.2 = (bf16[4,32,4096]{2,1,0:T(8,128)(2,1)S(1)}, bf16[4,32,4096]{2,1,0:T(8,128)(2,1)}, u32[]{:S(2)}, u32[]{:S(2)}) collective-permute-start(bf16[4,32,4096]{2,1,0:T(8,128)(2,1)S(1)} %collective-permute-done.1), channel_id=1, source_target_pairs={{4,0},{8,4},{12,8},{5,1},{9,5},{13,9},{6,2},{10,6},{14,10},{7,3},{... | collective-permute-start | bytes 3145736 | tf_op jit(solution)/shard_map/ppermute | solution.py:38
  36.1 26.3 %collective-permute-start.4 = (bf16[4,32,4096]{2,1,0:T(8,128)(2,1)S(1)}, bf16[4,32,4096]{2,1,0:T(8,128)(2,1)S(1)}, u32[]{:S(2)}, u32[]{:S(2)}) collective-permute-start(bf16[4,32,4096]{2,1,0:T(8,128)(2,1)S(1)} %collective-permute-done), channel_id=1, source_target_pairs={{0,4},{4,8},{8,12},{1,5},{5,9},{9,13},{2,6},{6,10},{10,14},{3,7},{... | collective-permute-start | bytes 3145736 | tf_op jit(solution)/shard_map/ppermute | solution.py:37
  40.8 288.1 %all-gather.5.cloned.1.call-start = ((), (), s32[]{:S(2)}) async-start(), calls=%async_computation.1 | async-start | bytes 11010048 | tf_op jit(solution)/shard_map/all_gather | solution.py:70
  61.2 25.6 %collective-permute-start.3 = (bf16[4,32,4096]{2,1,0:T(8,128)(2,1)}, bf16[4,32,4096]{2,1,0:T(8,128)(2,1)}, u32[]{:S(2)}, u32[]{:S(2)}) collective-permute-start(bf16[4,32,4096]{2,1,0:T(8,128)(2,1)} %collective-permute-done.2), channel_id=1, source_target_pairs={{4,0},{8,4},{12,8},{5,1},{9,5},{13,9},{6,2},{10,6},{14,10},{7,3},{... | collective-permute-start | bytes 3145736 | tf_op jit(solution)/shard_map/ppermute | solution.py:38
  62.5 25.7 %collective-permute-start.5 = (bf16[4,32,4096]{2,1,0:T(8,128)(2,1)S(1)}, bf16[4,32,4096]{2,1,0:T(8,128)(2,1)S(1)}, u32[]{:S(2)}, u32[]{:S(2)}) collective-permute-start(bf16[4,32,4096]{2,1,0:T(8,128)(2,1)S(1)} %collective-permute-done.4), channel_id=1, source_target_pairs={{0,4},{4,8},{8,12},{1,5},{5,9},{9,13},{2,6},{6,10},{10,14},{3,7},{... | collective-permute-start | bytes 3145736 | tf_op jit(solution)/shard_map/ppermute | solution.py:37
  96.1 26.3 %collective-permute-start.6 = (bf16[512,1024]{1,0:T(8,128)(2,1)}, bf16[512,1024]{1,0:T(8,128)(2,1)S(1)}, u32[]{:S(2)}, u32[]{:S(2)}) collective-permute-start(bf16[512,1024]{1,0:T(8,128)(2,1)} %get-tuple-element.25), channel_id=1, source_target_pairs={{0,2},{2,0},{1,3},{3,1},{4,6},{6,4},{5,7},{7,5},{8,10},{10,8},{9,1... | collective-permute-start | bytes 3145736 | tf_op jit(solution)/shard_map/ppermute | solution.py:85
  97.1 100.5 %collective-permute-start.20 = (bf16[4,64,7168]{2,1,0:T(8,128)(2,1)}, bf16[4,64,7168]{2,1,0:T(8,128)(2,1)}, u32[]{:S(2)}, u32[]{:S(2)}) collective-permute-start(bf16[4,64,7168]{2,1,0:T(8,128)(2,1)} %param.5), channel_id=1, source_target_pairs={{0,2},{2,0},{1,3},{3,1},{4,6},{6,4},{5,7},{7,5},{8,10},{10,8},{9,1... | collective-permute-start | bytes 11010056 | tf_op jit(solution)/shard_map/ppermute | solution.py:66
  130.8 66.7 %collective-permute-start.7 = (bf16[4,128,1024]{1,2,0:T(8,128)(2,1)S(1)}, bf16[4,128,1024]{1,2,0:T(8,128)(2,1)}, u32[]{:S(2)}, u32[]{:S(2)}) collective-permute-start(bf16[4,128,1024]{1,2,0:T(8,128)(2,1)S(1)} %maximum_multiply_fusion), channel_id=1, source_target_pairs={{0,1},{1,0},{2,3},{3,2},{4,5},{5,4},{6,7},{7,6},{8,9},{9,8},{10,11... | collective-permute-start | bytes 3145736 | tf_op jit(solution)/shard_map/ppermute | solution.py:48
  168.5 38.7 %collective-permute-start.11 = (bf16[128,3584]{1,0:T(8,128)(2,1)}, bf16[128,3584]{1,0:T(8,128)(2,1)}, u32[]{:S(2)}, u32[]{:S(2)}) collective-permute-start(bf16[128,3584]{1,0:T(8,128)(2,1)} %convert_element_type.137), channel_id=1, source_target_pairs={{0,4},{12,8},{1,5},{13,9},{2,6},{14,10},{3,7},{15,11},{16,20},{28,... | collective-permute-start | bytes 2752520 | tf_op jit(solution)/shard_map/ppermute | solution.py:20
  202.4 22.8 %collective-permute-start.14 = (bf16[128,3584]{1,0:T(8,128)(2,1)S(1)}, bf16[128,3584]{1,0:T(8,128)(2,1)S(1)}, u32[]{:S(2)}, u32[]{:S(2)}) collective-permute-start(bf16[128,3584]{1,0:T(8,128)(2,1)S(1)} %convert_element_type.142), channel_id=1, source_target_pairs={{0,4},{12,8},{1,5},{13,9},{2,6},{14,10},{3,7},{15,11},{16,20},{28,... | collective-permute-start | bytes 2752520 | tf_op jit(solution)/shard_map/ppermute | solution.py:20
  204.5 40.4 %collective-permute-start.8 = (bf16[128,3584]{1,0:T(8,128)(2,1)S(1)}, bf16[128,3584]{1,0:T(8,128)(2,1)S(1)}, u32[]{:S(2)}, u32[]{:S(2)}) collective-permute-start(bf16[128,3584]{1,0:T(8,128)(2,1)S(1)} %convert_element_type.132), channel_id=1, source_target_pairs={{0,4},{12,8},{1,5},{13,9},{2,6},{14,10},{3,7},{15,11},{16,20},{28,... | collective-permute-start | bytes 2752520 | tf_op jit(solution)/shard_map/ppermute | solution.py:20
  205.8 54.0 %collective-permute-start.17 = (bf16[128,3584]{1,0:T(8,128)(2,1)S(1)}, bf16[128,3584]{1,0:T(8,128)(2,1)S(1)}, u32[]{:S(2)}, u32[]{:S(2)}) collective-permute-start(bf16[128,3584]{1,0:T(8,128)(2,1)S(1)} %convert_element_type.147), channel_id=1, source_target_pairs={{0,4},{12,8},{1,5},{13,9},{2,6},{14,10},{3,7},{15,11},{16,20},{28,... | collective-permute-start | bytes 2752520 | tf_op jit(solution)/shard_map/ppermute | solution.py:20
  208.8 52.0 %collective-permute-start.12 = (bf16[128,3584]{1,0:T(8,128)(2,1)S(1)}, bf16[128,3584]{1,0:T(8,128)(2,1)S(1)}, u32[]{:S(2)}, u32[]{:S(2)}) collective-permute-start(bf16[128,3584]{1,0:T(8,128)(2,1)S(1)} %fusion.7), channel_id=1, source_target_pairs={{4,8},{8,4},{5,9},{9,5},{6,10},{10,6},{7,11},{11,7},{20,24},{24,20... | collective-permute-start | bytes 2752520 | tf_op jit(solution)/shard_map/ppermute | solution.py:22
  225.4 38.2 %collective-permute-start.15 = (bf16[128,3584]{1,0:T(8,128)(2,1)S(1)}, bf16[128,3584]{1,0:T(8,128)(2,1)S(1)}, u32[]{:S(2)}, u32[]{:S(2)}) collective-permute-start(bf16[128,3584]{1,0:T(8,128)(2,1)S(1)} %fusion.8), channel_id=1, source_target_pairs={{4,8},{8,4},{5,9},{9,5},{6,10},{10,6},{7,11},{11,7},{20,24},{24,20... | collective-permute-start | bytes 2752520 | tf_op jit(solution)/shard_map/ppermute | solution.py:22
  245.0 20.2 %collective-permute-start.9 = (bf16[128,3584]{1,0:T(8,128)(2,1)S(1)}, bf16[128,3584]{1,0:T(8,128)(2,1)S(1)}, u32[]{:S(2)}, u32[]{:S(2)}) collective-permute-start(bf16[128,3584]{1,0:T(8,128)(2,1)S(1)} %fusion.6), channel_id=1, source_target_pairs={{4,8},{8,4},{5,9},{9,5},{6,10},{10,6},{7,11},{11,7},{20,24},{24,20... | collective-permute-start | bytes 2752520 | tf_op jit(solution)/shard_map/ppermute | solution.py:22
  262.3 27.1 %collective-permute-start.13 = (bf16[128,3584]{1,0:T(8,128)(2,1)S(1)}, bf16[128,3584]{1,0:T(8,128)(2,1)S(1)}, u32[]{:S(2)}, u32[]{:S(2)}) collective-permute-start(bf16[128,3584]{1,0:T(8,128)(2,1)S(1)} %add_convert_fusion.7), channel_id=1, source_target_pairs={{4,0},{8,12},{5,1},{9,13},{6,2},{10,14},{7,3},{11,15},{20,16},{24,... | collective-permute-start | bytes 2752520 | tf_op jit(solution)/shard_map/ppermute | solution.py:26
  263.9 45.2 %collective-permute-start.16 = (bf16[128,3584]{1,0:T(8,128)(2,1)S(1)}, bf16[128,3584]{1,0:T(8,128)(2,1)S(1)}, u32[]{:S(2)}, u32[]{:S(2)}) collective-permute-start(bf16[128,3584]{1,0:T(8,128)(2,1)S(1)} %add_convert_fusion.6), channel_id=1, source_target_pairs={{4,0},{8,12},{5,1},{9,13},{6,2},{10,14},{7,3},{11,15},{20,16},{24,... | collective-permute-start | bytes 2752520 | tf_op jit(solution)/shard_map/ppermute | solution.py:26
  265.5 63.2 %collective-permute-start.10 = (bf16[128,3584]{1,0:T(8,128)(2,1)S(1)}, bf16[128,3584]{1,0:T(8,128)(2,1)S(1)}, u32[]{:S(2)}, u32[]{:S(2)}) collective-permute-start(bf16[128,3584]{1,0:T(8,128)(2,1)S(1)} %add_convert_fusion.8), channel_id=1, source_target_pairs={{4,0},{8,12},{5,1},{9,13},{6,2},{10,14},{7,3},{11,15},{20,16},{24,... | collective-permute-start | bytes 2752520 | tf_op jit(solution)/shard_map/ppermute | solution.py:26
  268.0 95.6 %collective-permute-start.19 = (bf16[128,3584]{1,0:T(8,128)(2,1)}, bf16[128,3584]{1,0:T(8,128)(2,1)}, u32[]{:S(2)}, u32[]{:S(2)}) collective-permute-start(bf16[128,3584]{1,0:T(8,128)(2,1)} %add_convert_fusion.5), channel_id=1, source_target_pairs={{4,0},{8,12},{5,1},{9,13},{6,2},{10,14},{7,3},{11,15},{20,16},{24,... | collective-permute-start | bytes 2752520 | tf_op jit(solution)/shard_map/ppermute | solution.py:26
  362.1 22.2 %collective-permute-start.24 = (bf16[128,3584]{1,0:T(8,128)(2,1)S(1)}, bf16[128,3584]{1,0:T(8,128)(2,1)S(1)}, u32[]{:S(2)}, u32[]{:S(2)}) collective-permute-start(bf16[128,3584]{1,0:T(8,128)(2,1)S(1)} %convert_element_type.157), channel_id=1, source_target_pairs={{0,4},{12,8},{1,5},{13,9},{2,6},{14,10},{3,7},{15,11},{16,20},{28,... | collective-permute-start | bytes 2752520 | tf_op jit(solution)/shard_map/ppermute | solution.py:20
  365.2 38.8 %collective-permute-start.27 = (bf16[128,3584]{1,0:T(8,128)(2,1)S(1)}, bf16[128,3584]{1,0:T(8,128)(2,1)S(1)}, u32[]{:S(2)}, u32[]{:S(2)}) collective-permute-start(bf16[128,3584]{1,0:T(8,128)(2,1)S(1)} %convert_element_type.162), channel_id=1, source_target_pairs={{0,4},{12,8},{1,5},{13,9},{2,6},{14,10},{3,7},{15,11},{16,20},{28,... | collective-permute-start | bytes 2752520 | tf_op jit(solution)/shard_map/ppermute | solution.py:20
  366.6 54.6 %collective-permute-start.21 = (bf16[128,3584]{1,0:T(8,128)(2,1)S(1)}, bf16[128,3584]{1,0:T(8,128)(2,1)S(1)}, u32[]{:S(2)}, u32[]{:S(2)}) collective-permute-start(bf16[128,3584]{1,0:T(8,128)(2,1)S(1)} %convert_element_type.152), channel_id=1, source_target_pairs={{0,4},{12,8},{1,5},{13,9},{2,6},{14,10},{3,7},{15,11},{16,20},{28,... | collective-permute-start | bytes 2752520 | tf_op jit(solution)/shard_map/ppermute | solution.py:20
  367.9 63.1 %collective-permute-start.30 = (bf16[128,3584]{1,0:T(8,128)(2,1)S(1)}, bf16[128,3584]{1,0:T(8,128)(2,1)S(1)}, u32[]{:S(2)}, u32[]{:S(2)}) collective-permute-start(bf16[128,3584]{1,0:T(8,128)(2,1)S(1)} %convert_element_type.167), channel_id=1, source_target_pairs={{0,4},{12,8},{1,5},{13,9},{2,6},{14,10},{3,7},{15,11},{16,20},{28,... | collective-permute-start | bytes 2752520 | tf_op jit(solution)/shard_map/ppermute | solution.py:20
  384.5 47.4 %collective-permute-start.25 = (bf16[128,3584]{1,0:T(8,128)(2,1)S(1)}, bf16[128,3584]{1,0:T(8,128)(2,1)S(1)}, u32[]{:S(2)}, u32[]{:S(2)}) collective-permute-start(bf16[128,3584]{1,0:T(8,128)(2,1)S(1)} %fusion.11), channel_id=1, source_target_pairs={{4,8},{8,4},{5,9},{9,5},{6,10},{10,6},{7,11},{11,7},{20,24},{24,20... | collective-permute-start | bytes 2752520 | tf_op jit(solution)/shard_map/ppermute | solution.py:22
  404.1 29.3 %collective-permute-start.28 = (bf16[128,3584]{1,0:T(8,128)(2,1)S(1)}, bf16[128,3584]{1,0:T(8,128)(2,1)S(1)}, u32[]{:S(2)}, u32[]{:S(2)}) collective-permute-start(bf16[128,3584]{1,0:T(8,128)(2,1)S(1)} %fusion.12), channel_id=1, source_target_pairs={{4,8},{8,4},{5,9},{9,5},{6,10},{10,6},{7,11},{11,7},{20,24},{24,20... | collective-permute-start | bytes 2752520 | tf_op jit(solution)/shard_map/ppermute | solution.py:22
  432.2 27.6 %collective-permute-start.26 = (bf16[128,3584]{1,0:T(8,128)(2,1)S(1)}, bf16[128,3584]{1,0:T(8,128)(2,1)S(1)}, u32[]{:S(2)}, u32[]{:S(2)}) collective-permute-start(bf16[128,3584]{1,0:T(8,128)(2,1)S(1)} %add_convert_fusion.3), channel_id=1, source_target_pairs={{4,0},{8,12},{5,1},{9,13},{6,2},{10,14},{7,3},{11,15},{20,16},{24,... | collective-permute-start | bytes 2752520 | tf_op jit(solution)/shard_map/ppermute | solution.py:26
  433.8 45.7 %collective-permute-start.29 = (bf16[128,3584]{1,0:T(8,128)(2,1)S(1)}, bf16[128,3584]{1,0:T(8,128)(2,1)S(1)}, u32[]{:S(2)}, u32[]{:S(2)}) collective-permute-start(bf16[128,3584]{1,0:T(8,128)(2,1)S(1)} %add_convert_fusion.2), channel_id=1, source_target_pairs={{4,0},{8,12},{5,1},{9,13},{6,2},{10,14},{7,3},{11,15},{20,16},{24,... | collective-permute-start | bytes 2752520 | tf_op jit(solution)/shard_map/ppermute | solution.py:26
  435.6 60.4 %collective-permute-start.23 = (bf16[128,3584]{1,0:T(8,128)(2,1)S(1)}, bf16[128,3584]{1,0:T(8,128)(2,1)S(1)}, u32[]{:S(2)}, u32[]{:S(2)}) collective-permute-start(bf16[128,3584]{1,0:T(8,128)(2,1)S(1)} %add_convert_fusion.4), channel_id=1, source_target_pairs={{4,0},{8,12},{5,1},{9,13},{6,2},{10,14},{7,3},{11,15},{20,16},{24,... | collective-permute-start | bytes 2752520 | tf_op jit(solution)/shard_map/ppermute | solution.py:26
  437.2 68.7 %collective-permute-start.32 = (bf16[128,3584]{1,0:T(8,128)(2,1)S(1)}, bf16[128,3584]{1,0:T(8,128)(2,1)S(1)}, u32[]{:S(2)}, u32[]{:S(2)}) collective-permute-start(bf16[128,3584]{1,0:T(8,128)(2,1)S(1)} %add_convert_fusion.1), channel_id=1, source_target_pairs={{4,0},{8,12},{5,1},{9,13},{6,2},{10,14},{7,3},{11,15},{20,16},{24,... | collective-permute-start | bytes 2752520 | tf_op jit(solution)/shard_map/ppermute | solution.py:26
  (10 other events, 63.3 us)
Sparse Core Ops, SparseCore 0:
  40.9 19.6 all-gather.2
  197.7 18.1 all-gather.4
